TPU v7x, 128 devices: a whole 4x4x4 slice. The times are simulated.
128 devices in a mesh: row: 8 (over x, core), col: 16 (over y, z).
Axes of the slice: x: 4, y: 4, z: 4, core: 2. Of those that a mesh axis runs over, the one named last changes fastest.
Arguments:
- amplitudes: float32 [256, 32768], P(('row', 'col')), may hold values from -6 to 6
- integrals: float32 [16384, 32768], P('row', 'col'), may hold values from -0.09375 to 0.09375
- ij_irrep: int32 [256], replicated, may hold values from 0 to 7
- ab_irrep: int32 [16384], P('row'), may hold values from 0 to 7
- cd_irrep: int32 [32768], P('col'), may hold values from 0 to 7
Outputs:
- ladder_out: float32 [256, 16384], P(('row', 'col'))
All inputs are finite; a program needn't handle non-finite values.
Results may differ from a plain program's by a relative error of at most 0.000078.
Values sent between devices are 32-bit elements; how exact they have to be, the bound alone decides.
A program may use at most 64 MiB of HBM per device.

v0:
```python
import jax
import jax.numpy as jnp
from jax import lax
from jax.sharding import PartitionSpec as P


def contract(amp_block, integrals):
    return lax.dot_general(
        amp_block,
        integrals,
        (((1,), (1,)), ((), ())),
        precision=lax.Precision.HIGHEST,
        preferred_element_type=jnp.float32,
    )


def body(amplitudes, integrals, ij_irrep, ab_irrep, cd_irrep):
    by_column = lax.all_to_all(amplitudes, "col", split_axis=1, concat_axis=0, tiled=True)
    gathered = lax.all_gather(by_column, "row", axis=0, tiled=True)
    row_count = lax.axis_size("row")
    col_count = lax.axis_size("col")
    pair_count = gathered.shape[0]
    col_width = gathered.shape[1]
    own_pairs = pair_count // (row_count * col_count)
    ordered = (
        gathered.reshape(row_count, col_count, own_pairs, col_width)
        .transpose(1, 0, 2, 3)
        .reshape(pair_count, col_width)
    )
    pair_irrep = (
        ij_irrep.reshape(row_count, col_count, own_pairs).transpose(1, 0, 2).reshape(pair_count)
    )
    masked = jnp.where(cd_irrep[None, :] == pair_irrep[:, None], ordered, 0.0)
    product = contract(masked, integrals)
    shared = lax.psum_scatter(
        jnp.where(pair_irrep[:, None] == ab_irrep[None, :], product, 0.0),
        "col",
        scatter_dimension=0,
        tiled=True,
    )
    owned = lax.all_to_all(shared, "row", split_axis=0, concat_axis=1, tiled=True)
    return owned


def solution(mesh):
    in_specs = (P(("row", "col"), None), P("row", "col"), P(), P("row"), P("col"))
    out_specs = P(("row", "col"), None)
    return jax.shard_map(body, mesh=mesh, in_specs=in_specs, out_specs=out_specs, check_vma=False)
```

profile of v0, /device:TPU:1, one launch (start us, length us, event | category | flops | bytes accessed | tf_op | source)
XLA Modules:
  0.0 166.6 jit_solution(9258753089181089107)
XLA Ops:
  6.5 0.0 all-gather.2.cloned.1.call-start
  6.5 16.1 %all_to_all.38 = f32[2,16,2048]{2,0,1:T(2,128)S(1)} all-to-all(f32[2,16,2048]{2,0,1:T(2,128)} %bitcast.11), channel_id=1, replica_groups=mesh['row'=8,'col'=16] {'col'}, dimensions={1} | all-to-all | bytes 524288 | tf_op jit(solution)/shard_map/all_to_all | solution.py:18
  22.6 0.9 all_to_all.31
  23.5 0.0 all-gather.2.cloned.1.call-update
  23.5 0.0 reduce-scatter.2.cloned.1.call-start
  23.6 0.8 reshape.18
  24.4 0.1 eq.12
  24.5 24.0 %all-gather.2.cloned.1.call-done = f32[256,2048]{1,0:T(8,128)} async-done(((f32[32,2048]{1,0:T(8,128)}), f32[256,2048]{1,0:T(8,128)}) %all-gather.2.cloned.1.call-update) | async-done | bytes 2097168 | tf_op jit(solution)/shard_map/all_gather | solution.py:19
  48.5 2.5 %reshape.19 = f32[8,16,2,2048]{3,2,1,0:T(2,128)S(1)} reshape(f32[256,2048]{1,0:T(8,128)} %all-gather.2.cloned.1.call-done) | data formatting | bytes 4194304 | tf_op jit(solution)/shard_map/reshape | solution.py:26
  51.0 1.6 copy.9
  52.6 0.0 copy-start
  52.6 0.0 copy-start.1
  52.6 2.7 %reshape.20 = f32[256,2048]{1,0:T(8,128)S(1)} reshape(f32[16,8,2,2048]{3,2,1,0:T(2,128)} %copy.9) | data formatting | bytes 4194304 | tf_op jit(solution)/shard_map/reshape | solution.py:28
  55.3 0.0 copy-done
  55.3 0.0 copy-done.1
  55.3 18.1 %convolution_select_fusion = f32[256,2048]{1,0:T(8,128)} fusion(f32[2048,2048]{1,0:T(8,128)} %param.6, f32[256,2048]{1,0:T(8,128)S(1)} %reshape.20, s32[2048]{0:T(1024)S(1)} %copy-done, s32[2048]{0:T(1024)S(1)} %copy-done.1, s32[256]{0:T(256)S(1)} %eq.12), kind=kOutput, calls=%fused_computation | convolution fusion | flops 12886999040 | bytes 20988928 | tf_op jit(solution)/shard_map/dot_general | solution.py:8
  73.5 0.0 reduce-scatter.2.cloned.1.call-update
  73.5 73.0 %reduce-scatter.2.cloned.1.call-done = f32[16,2048]{1,0:T(8,128)} async-done(((f32[256,2048]{1,0:T(8,128)}), f32[16,2048]{1,0:T(8,128)}) %reduce-scatter.2.cloned.1.call-update) | async-done | bytes 131088 | tf_op jit(solution)/shard_map/reduce_scatter | solution.py:35
  146.5 1.0 all_to_all.32
  147.5 11.6 %all_to_all.39 = f32[8,2,2048]{2,1,0:T(2,128)S(1)} all-to-all(f32[8,2,2048]{2,1,0:T(2,128)S(1)} %all_to_all.32), channel_id=1, replica_groups=mesh['row'=8,'col'=16] {'row'}, dimensions={0} | all-to-all | bytes 262144 | tf_op jit(solution)/shard_map/all_to_all | solution.py:41
  159.1 0.7 copy.12
  (1 shorter events, 0.0 us)
Async XLA Ops:
  6.5 42.0 %all-gather.2.cloned.1.call-start = ((), (), s32[]{:S(2)}) async-start(), calls=%async_computation.3 | async-start | bytes 2359296 | tf_op jit(solution)/shard_map/all_gather | solution.py:19
  23.5 123.0 %reduce-scatter.2.cloned.1.call-start = ((), (), s32[]{:S(2)}) async-start(), calls=%async_computation.4 | async-start | bytes 2228224 | tf_op jit(solution)/shard_map/reduce_scatter | solution.py:35
  52.6 2.7 %copy-start = (s32[2048]{0:T(1024)S(1)}, s32[2048]{0:T(1024)}, u32[]{:S(2)}) copy-start(s32[2048]{0:T(1024)} %param.9) | copy-start | bytes 24580
  52.6 2.7 %copy-start.1 = (s32[2048]{0:T(1024)S(1)}, s32[2048]{0:T(1024)}, u32[]{:S(2)}) copy-start(s32[2048]{0:T(1024)} %param.8) | copy-start | bytes 24580
Sparse Core Ops, SparseCore 0:
  23.6 24.8 all-gather.1
  73.6 72.8 reduce-scatter.1
where the time goes:
time: 167 us
  waiting for transfers between devices  97 us (58%)
  blocking collectives  27.6 us (17%)
  matrix products  18.1 us (11%)
  between operations  13.5 us (8%)
  local copies, waits for them, and re-layouts  10.3 us (6%)
    reduce_scatter x1, waiting for transfers between devices, body(): lax.psum_scatter(jnp.where(pair_irrep[:, None] == ab_irrep[None, :], prod...  73 us
    all_gather x1, waiting for transfers between devices, body(): gathered = lax.all_gather(by_column, 'row', axis=0, tiled=True)  24 us
    dot_general x1, matrix products, contract(): lax.dot_general(amp_block, integrals, (((1,), (1,)), ((), ())), precision...  18.1 us
    all_to_all x1, blocking collectives, body(): lax.all_to_all(amplitudes, 'col', split_axis=1, concat_axis=0, tiled=True)  16.1 us
    all_to_all x1, blocking collectives, body(): lax.all_to_all(shared, 'row', split_axis=0, concat_axis=1, tiled=True)  11.6 us
  transfers between devices with their start and end apart: 2, of which 2 were waited for; matrix products, arithmetic and copies ran while one was open for 1% of the time, Pallas kernels for 0%

commit v1 on v0

--- a/solution.py
+++ b/solution.py
@@ -16,7 +16,15 @@
 
 def body(amplitudes, integrals, ij_irrep, ab_irrep, cd_irrep):
     by_column = lax.all_to_all(amplitudes, "col", split_axis=1, concat_axis=0, tiled=True)
-    gathered = lax.all_gather(by_column, "row", axis=0, tiled=True)
+    gathered = jnp.concatenate(
+        jax.lax.all_to_all(
+            jnp.stack([by_column] * jax.lax.axis_size("row"), axis=0),
+            axis_name="row",
+            split_axis=0,
+            concat_axis=0,
+        ),
+        axis=0,
+    )
     row_count = lax.axis_size("row")
     col_count = lax.axis_size("col")
     pair_count = gathered.shape[0]

time: 167 us -> 172 us (1.030)
  starting transfers between devices: 0.04 us -> 6.44 us
    all_to_all x0 -> x1, waiting for transfers between devices: none -> 26 us  [body(): jax.lax.all_to_all(jnp.stack([by_column] * jax.lax.axis_size('row'), axis...]
    all_gather x1 -> x0, waiting for transfers between devices: 24 us -> none  [body(): gathered = lax.all_gather(by_column, 'row', axis=0, tiled=True)]
    all_to_all x0 -> x1, starting transfers between devices: none -> 6.44 us  [body(): jax.lax.all_to_all(jnp.stack([by_column] * jax.lax.axis_size('row'), axis...]
    reduce_scatter x1, waiting for transfers between devices: 73 us -> 69.4 us  [body(): lax.psum_scatter(jnp.where(pair_irrep[:, None] == ab_irrep[None, :], prod...]
    reshape x1 -> x0, local copies, waits for them, and re-layouts: 2.49 us -> none  [body(): gathered.reshape(row_count, col_count, own_pairs, col_width)]
    another operation x0 -> x2, local copies, waits for them, and re-layouts: none -> 1.76 us  [body(): jnp.stack([by_column] * jax.lax.axis_size('row'), axis=0)]
  transfers between devices with their start and end apart: 2 -> 2, of which waited for: 2 -> 2; matrix products, arithmetic and copies ran while one was open for 1% -> 0% of each run, Pallas kernels for 0% -> 0%
where the time goes in v1:
time: 172 us
  waiting for transfers between devices  95.5 us (56%)
  blocking collectives  27.7 us (16%)
  matrix products  18.1 us (11%)
  between operations  13.4 us (8%)
  local copies, waits for them, and re-layouts  10.6 us (6%)
  starting transfers between devices  6.44 us (4%)
    reduce_scatter x1, waiting for transfers between devices, body(): lax.psum_scatter(jnp.where(pair_irrep[:, None] == ab_irrep[None, :], prod...  69.4 us
    all_to_all x1, waiting for transfers between devices, body(): jax.lax.all_to_all(jnp.stack([by_column] * jax.lax.axis_size('row'), axis...  26 us
    dot_general x1, matrix products, contract(): lax.dot_general(amp_block, integrals, (((1,), (1,)), ((), ())), precision...  18.1 us
    all_to_all x1, blocking collectives, body(): lax.all_to_all(amplitudes, 'col', split_axis=1, concat_axis=0, tiled=True)  16.1 us
    all_to_all x1, blocking collectives, body(): lax.all_to_all(shared, 'row', split_axis=0, concat_axis=1, tiled=True)  11.6 us
    all_to_all x1, starting transfers between devices, body(): jax.lax.all_to_all(jnp.stack([by_column] * jax.lax.axis_size('row'), axis...  6.44 us
  transfers between devices with their start and end apart: 2, of which 2 were waited for; matrix products, arithmetic and copies ran while one was open for 0% of the time, Pallas kernels for 0%

profile of v1, /device:TPU:1, one launch (start us, length us, event | category | flops | bytes accessed | tf_op | source)
XLA Modules:
  0.0 171.8 jit_solution(13993831416329387181)
XLA Ops:
  6.5 16.1 %all_to_all.40 = f32[2,16,2048]{2,0,1:T(2,128)S(1)} all-to-all(f32[2,16,2048]{2,0,1:T(2,128)} %bitcast.13), channel_id=1, replica_groups=mesh['row'=8,'col'=16] {'col'}, dimensions={1} | all-to-all | bytes 524288 | tf_op jit(solution)/shard_map/all_to_all | solution.py:18
  22.6 0.2 stack.4
  22.8 1.6 stack.5
  24.4 0.0 copy-start.2
  24.4 6.4 %all-to-all-start.1 = ((f32[8,32,2048]{2,1,0:T(8,128)}), f32[8,32,2048]{2,1,0:T(8,128)S(1)}, u32[]{:S(2)}, u32[]{:S(2)}) async-start(f32[8,32,2048]{2,1,0:T(8,128)} %stack.5), calls=%async_computation.1 | async-start | bytes 4194304 | tf_op jit(solution)/shard_map/all_to_all | solution.py:20
  30.8 0.0 reduce-scatter.2.cloned.1.call-start
  30.8 0.0 copy-done.2
  30.8 0.1 reshape.18
  31.0 0.1 eq.12
  31.1 26.0 %all-to-all-done.1 = f32[8,32,2048]{2,1,0:T(8,128)S(1)} async-done(((f32[8,32,2048]{2,1,0:T(8,128)}), f32[8,32,2048]{2,1,0:T(8,128)S(1)}, u32[]{:S(2)}, u32[]{:S(2)}) %all-to-all-start.1) | async-done | bytes 2097184 | tf_op jit(solution)/shard_map/all_to_all | solution.py:20
  57.1 1.2 copy.13
  58.4 3.0 %copy.14 = f32[16,8,2,2048]{3,2,1,0:T(2,128)} copy(f32[16,8,2,2048]{3,1,2,0:T(8,128)S(1)} %bitcast.10) | data formatting | bytes 4194304 | tf_op jit(solution)/shard_map/transpose | solution.py:35
  61.3 0.0 copy-start
  61.3 0.0 copy-start.1
  61.3 2.7 %reshape.19 = f32[256,2048]{1,0:T(8,128)S(1)} reshape(f32[16,8,2,2048]{3,2,1,0:T(2,128)} %copy.14) | data formatting | bytes 4194304 | tf_op jit(solution)/shard_map/reshape | solution.py:36
  64.1 0.0 copy-done
  64.1 0.0 copy-done.1
  64.1 18.1 %convolution_select_fusion = f32[256,2048]{1,0:T(8,128)} fusion(f32[2048,2048]{1,0:T(8,128)} %param.6, f32[256,2048]{1,0:T(8,128)S(1)} %reshape.19, s32[2048]{0:T(1024)S(1)} %copy-done, s32[2048]{0:T(1024)S(1)} %copy-done.1, s32[256]{0:T(256)S(1)} %eq.12), kind=kOutput, calls=%fused_computation | convolution fusion | flops 12886999040 | bytes 20988928 | tf_op jit(solution)/shard_map/dot_general | solution.py:8
  82.2 0.0 reduce-scatter.2.cloned.1.call-update
  82.2 69.4 %reduce-scatter.2.cloned.1.call-done = f32[16,2048]{1,0:T(8,128)} async-done(((f32[256,2048]{1,0:T(8,128)}), f32[16,2048]{1,0:T(8,128)}) %reduce-scatter.2.cloned.1.call-update) | async-done | bytes 131088 | tf_op jit(solution)/shard_map/reduce_scatter | solution.py:43
  151.7 1.0 all_to_all.33
  152.7 11.6 %all_to_all.41 = f32[8,2,2048]{2,1,0:T(2,128)S(1)} all-to-all(f32[8,2,2048]{2,1,0:T(2,128)S(1)} %all_to_all.33), channel_id=1, replica_groups=mesh['row'=8,'col'=16] {'row'}, dimensions={0} | all-to-all | bytes 262144 | tf_op jit(solution)/shard_map/all_to_all | solution.py:49
  164.3 0.7 copy.17
  (1 shorter events, 0.0 us)
Async XLA Ops:
  24.4 6.4 %copy-start.2 = (s32[256]{0:T(256)S(1)}, s32[256]{0:T(256)}, u32[]{:S(2)}) copy-start(s32[256]{0:T(256)} %param.7) | copy-start | bytes 3076
  24.4 32.8 %all-to-all-start.1 = ((f32[8,32,2048]{2,1,0:T(8,128)}), f32[8,32,2048]{2,1,0:T(8,128)S(1)}, u32[]{:S(2)}, u32[]{:S(2)}) async-start(f32[8,32,2048]{2,1,0:T(8,128)} %stack.5), calls=%async_computation.1 | async-start | bytes 4194304 | tf_op jit(solution)/shard_map/all_to_all | solution.py:20
  30.8 120.9 %reduce-scatter.2.cloned.1.call-start = ((), (), s32[]{:S(2)}) async-start(), calls=%async_computation.4 | async-start | bytes 2228224 | tf_op jit(solution)/shard_map/reduce_scatter | solution.py:43
  61.3 2.7 %copy-start = (s32[2048]{0:T(1024)S(1)}, s32[2048]{0:T(1024)}, u32[]{:S(2)}) copy-start(s32[2048]{0:T(1024)} %param.9) | copy-start | bytes 24580
  61.3 2.7 %copy-start.1 = (s32[2048]{0:T(1024)S(1)}, s32[2048]{0:T(1024)}, u32[]{:S(2)}) copy-start(s32[2048]{0:T(1024)} %param.8) | copy-start | bytes 24580
Sparse Core Ops, SparseCore 0:
  82.4 69.2 reduce-scatter.1
